TPU v7x, 128 devices: a whole 4x4x4 slice. The times are simulated.
128 devices in a mesh: row: 8 (over x, y_lo), col: 16 (over y_hi, z, core).
Axes of the slice: x: 4, y: 4 (y_hi: 2, y_lo: 2; y = y_hi * 2 + y_lo), z: 4, core: 2. Of those that a mesh axis runs over, the one named last changes fastest.
Arguments:
- front: float32 [10240, 10240], P('row', 'col'), as said below
- updates: float32 [16384, 8192], P('row', 'col'), as said below
- maps: int32 [2, 64], replicated, may hold values from 0 to 79, as said below
Outputs:
- panel_factor: float32 [10240, 2048], P('row', 'col')
- trailing: float32 [10240, 10240], P('row', 'col')
Inputs may be any that keep to these rules, and one draw needn't show every extreme that they name: `maps`: each row lists 64 distinct front blocks; entry j leaves remainder floor(j / 4) on division by 16, the entries of one remainder rise with j, and blocks 0 and 79 appear in both rows. Symmetric in front order; the assembled leading 2048 x 2048 block is positive definite. `updates`: each child's update is symmetric in the child's own order.
All inputs are finite; a program needn't handle non-finite values.
Results may differ from a plain program's by a relative error of at most 0.0001.
Values sent between devices are 32-bit elements; how exact they have to be, the bound alone decides.
No kernel may reach another device: no remote copies, remote signals or barrier semaphores. Data moves between devices by JAX's collectives and lax.ppermute only.
A program may use at most 192 MiB of HBM per device.

v0:
```python
import jax
import jax.numpy as jnp
from jax import lax
from jax.sharding import PartitionSpec as P

BLK = 128
PW = 2048


def from_root(value, axis, source):
    kept = jnp.where(lax.axis_index(axis) == source, value, 0).astype(value.dtype)
    return lax.psum(kept, axis)


def block_cholesky(leading):
    order = leading.shape[0]
    count = order // BLK
    identity = jnp.eye(BLK, dtype=jnp.float32)
    factor = jnp.zeros((order, order), jnp.float32)
    inverses = []
    for step in range(count):
        start = step * BLK
        column = leading[start:, start : start + BLK]
        if step > 0:
            column = column - jnp.dot(
                factor[start:, :start],
                factor[start : start + BLK, :start].T,
                precision=lax.Precision.HIGHEST,
                preferred_element_type=jnp.float32,
            )
        diag_factor = jnp.linalg.cholesky(column[:BLK])
        inverse = jax.scipy.linalg.solve_triangular(diag_factor, identity, lower=True)
        inverses.append(inverse)
        factor = factor.at[start : start + BLK, start : start + BLK].set(diag_factor)
        if start + BLK < order:
            below = jnp.dot(
                column[BLK:],
                inverse.T,
                precision=lax.Precision.HIGHEST,
                preferred_element_type=jnp.float32,
            )
            factor = factor.at[start + BLK :, start : start + BLK].set(below)
    return (factor, inverses)


def block_solve(factor, inverses, rows_in):
    count = len(inverses)
    result = jnp.zeros(rows_in.shape, jnp.float32)
    for step in range(count):
        start = step * BLK
        target = rows_in[:, start : start + BLK]
        if step > 0:
            target = target - jnp.dot(
                result[:, :start],
                factor[start : start + BLK, :start].T,
                precision=lax.Precision.HIGHEST,
                preferred_element_type=jnp.float32,
            )
        solved = jnp.dot(
            target,
            inverses[step].T,
            precision=lax.Precision.HIGHEST,
            preferred_element_type=jnp.float32,
        )
        result = result.at[:, start : start + BLK].set(solved)
    return result


def local(front, updates, maps):
    rows_n = lax.axis_size("row")
    cols_n = lax.axis_size("col")
    half_rows = rows_n // 2
    row_at = lax.axis_index("row")
    col_at = lax.axis_index("col")
    front_rows, front_cols = front.shape
    row_slots = front_rows // BLK
    col_slots = front_cols // BLK
    col_group = updates.shape[1] // BLK
    depth_slots = col_group // half_rows
    width_slots = cols_n // rows_n
    child_blocks = maps.shape[1]
    outgoing = updates.reshape(width_slots, rows_n, depth_slots * BLK, col_group * BLK)
    incoming = lax.all_to_all(outgoing, "row", split_axis=1, concat_axis=1, tiled=True)
    incoming = incoming.reshape(width_slots, 2, half_rows, depth_slots, BLK, col_group, BLK)
    shape_grid = (width_slots, half_rows, depth_slots)
    grid_w = lax.broadcasted_iota(jnp.int32, shape_grid, 0)
    grid_a = lax.broadcasted_iota(jnp.int32, shape_grid, 1)
    grid_e = lax.broadcasted_iota(jnp.int32, shape_grid, 2)
    block_id = (((grid_w * rows_n + row_at) * depth_slots + grid_e) * half_rows + grid_a).reshape(
        -1
    )
    child_iota = jnp.arange(child_blocks, dtype=jnp.int32)
    assembled = front
    for which_child in range(2):
        child_map = maps[which_child]
        blocks = incoming[:, which_child].reshape(
            width_slots * half_rows * depth_slots, BLK, col_group, BLK
        )
        matched = block_id[:, None] == child_iota[None, :]
        targets = jnp.sum(jnp.where(matched, child_map[None, :], 0), axis=1)
        row_place = (
            targets[None, :] // rows_n == jnp.arange(row_slots, dtype=jnp.int32)[:, None]
        ).astype(jnp.float32)
        col_ids = lax.dynamic_slice_in_dim(child_map, col_at * col_group, col_group)
        col_place = (
            col_ids[None, :] // cols_n == jnp.arange(col_slots, dtype=jnp.int32)[:, None]
        ).astype(jnp.float32)
        placed = jnp.einsum("pn,nxvy->pxvy", row_place, blocks, precision=lax.Precision.HIGHEST)
        placed = jnp.einsum("pxvy,qv->pxqy", placed, col_place, precision=lax.Precision.HIGHEST)
        assembled = assembled + placed.reshape(front_rows, front_cols)
    panel_rslots = PW // BLK // rows_n
    panel_cslots = PW // BLK // cols_n
    gathered = lax.all_gather(assembled[:, : panel_cslots * BLK], "col", axis=1, tiled=True)
    panel_rows = (
        gathered.reshape(front_rows, cols_n, panel_cslots, BLK)
        .transpose(0, 2, 1, 3)
        .reshape(front_rows, PW)
    )
    corner = assembled[: panel_rslots * BLK, : panel_cslots * BLK]
    pieces = lax.all_gather(corner, ("row", "col"), axis=0, tiled=True)
    leading = (
        pieces.reshape(rows_n, cols_n, panel_rslots, BLK, panel_cslots, BLK)
        .transpose(2, 0, 3, 4, 1, 5)
        .reshape(PW, PW)
    )
    factor, inverses = block_cholesky(leading)
    lower_rows = block_solve(factor, inverses, panel_rows[panel_rslots * BLK :])
    head_rows = lax.dynamic_index_in_dim(
        factor.reshape(panel_rslots, rows_n, BLK, PW), row_at, 1, keepdims=False
    )
    factor_rows = jnp.concatenate([head_rows.reshape(panel_rslots * BLK, PW), lower_rows], axis=0)
    col_span = cols_n // rows_n
    root_row = col_at % rows_n
    picked = lax.dynamic_index_in_dim(
        factor_rows.reshape(col_slots, col_span, BLK, PW), col_at // rows_n, 1, keepdims=False
    )
    column_rows = from_root(picked.reshape(col_slots * BLK, PW), "row", root_row)
    update = jnp.dot(
        factor_rows,
        column_rows.T,
        precision=lax.Precision.HIGHEST,
        preferred_element_type=jnp.float32,
    )
    row_keep = jnp.arange(front_rows) // BLK >= panel_rslots
    col_keep = jnp.arange(front_cols) // BLK >= panel_cslots
    trailing = jnp.where(
        row_keep[:, None] & col_keep[None, :], assembled - update, jnp.float32(0.0)
    )
    panel_out = lax.dynamic_index_in_dim(
        factor_rows.reshape(front_rows, panel_cslots, cols_n, BLK), col_at, 2, keepdims=False
    )
    return (panel_out.reshape(front_rows, panel_cslots * BLK), trailing)


def solution(mesh):
    in_specs = (P("row", "col"), P("row", "col"), P())
    out_specs = (P("row", "col"), P("row", "col"))
    return jax.shard_map(local, mesh=mesh, in_specs=in_specs, out_specs=out_specs, check_vma=False)
```

profile of v0, /device:TPU:1, one launch (start us, length us, event | category | flops | bytes accessed | tf_op | source)
XLA Modules:
  0.0 1348.0 jit_solution(4815525074434272048)
XLA Ops:
  18.3 58.4 %all-to-all-done = f32[2,8,128,512]{3,2,0,1:T(8,128)} async-done(((f32[2,8,128,512]{3,2,0,1:T(8,128)}), f32[2,8,128,512]{3,2,0,1:T(8,128)}, u32[]{:S(2)}, u32[]{:S(2)}) %all-to-all-start) | async-done | bytes 4194336 | tf_op jit(solution)/shard_map/all_to_all | solution.py:83
  108.5 208.8 %all-gather.3.cloned.1.call-done = f32[32768,128]{1,0:T(8,128)} async-done(((f32[256,128]{1,0:T(8,128)}), f32[32768,128]{1,0:T(8,128)}) %all-gather.3.cloned.1.call-update) | async-done | bytes 16777232 | tf_op jit(solution)/shard_map/all_gather | solution.py:120
  317.3 17.8 %copy.161 = f32[8,16,2,128,1,128]{3,0,2,5,1,4:T(8,128)} copy(f32[8,16,2,128,1,128]{5,3,2,1,0,4:T(8,128)} %bitcast.269) | data formatting | bytes 33554432 | tf_op jit(solution)/shard_map/reshape | solution.py:122
  335.1 18.0 %reshape.1456 = f32[2048,2048]{0,1:T(8,128)} reshape(f32[2,8,128,1,16,128]{2,1,0,5,4,3:T(8,128)} %bitcast.263) | data formatting | bytes 33554432 | tf_op jit(solution)/shard_map/reshape | solution.py:124
  354.9 11.7 cholesky.254
  392.2 11.9 cholesky.265
  422.7 11.7 cholesky.276
  454.1 11.7 cholesky.287
  486.3 11.7 cholesky.298
  518.4 11.7 cholesky.309
  551.2 11.7 cholesky.320
  583.7 12.1 cholesky.331
  616.8 11.9 cholesky.342
  648.9 11.9 cholesky.353
  681.0 11.7 cholesky.364
  773.1 11.9 cholesky.397
  975.4 12.6 fusion.72
  991.0 13.4 fusion.75
  1007.5 14.3 %fusion.125 = f32[1024,128]{1,0:T(8,128)S(1)} fusion(f32[1024,2048]{0,1:T(8,128)} %fusion.100, f32[2048,2048]{1,0:T(8,128)} %get-tuple-element.575, f32[1280,2048]{1,0:T(8,128)S(1)} %bitcast.274), kind=kOutput, calls=%fused_computation.126 | convolution fusion | flops 2818703360 | bytes 9306112 | tf_op jit(solution)/shard_map/dot_general | solution.py:53
  1023.3 14.4 %fusion.78 = f32[1024,128]{1,0:T(8,128)S(1)} fusion(f32[1024,2048]{0,1:T(8,128)S(1)} %fusion.99, f32[2048,2048]{1,0:T(8,128)} %get-tuple-element.575, f32[1280,2048]{1,0:T(8,128)S(1)} %bitcast.274), kind=kOutput, calls=%fused_computation.84 | convolution fusion | flops 3020029952 | bytes 9895936 | tf_op jit(solution)/shard_map/dot_general | solution.py:53
  1048.1 13.3 reshape.1460
  1061.3 21.0 %fusion.10 = f32[5,128,2048]{1,0,2:T(8,128)} fusion(pred[]{:T(512)S(6)} %eq.132, f32[5,2,128,2048]{2,1,0,3:T(2,128)} %reshape.1460, s32[]{:T(128)S(6)} %select_n.110), kind=kLoop, calls=%fused_computation.14 | loop fusion | flops 1310720 | bytes 10485765 | tf_op jit(solution)/shard_map/jit(_where)/select_n | solution.py:11
  1098.3 211.5 %all-reduce.4.cloned.1.call-done = f32[640,2048]{0,1:T(8,128)} async-done(((f32[640,2048]{0,1:T(8,128)}), f32[640,2048]{0,1:T(8,128)}) %all-reduce.4.cloned.1.call-update) | async-done | bytes 5242896 | tf_op jit(solution)/shard_map/psum | solution.py:12
  1309.8 31.6 %fusion.33 = f32[1280,640]{1,0:T(8,128)} fusion(f32[1280,640]{1,0:T(8,128)} %copy-done.5, f32[640,2048]{0,1:T(8,128)} %all-reduce.4.cloned.1.call-done, pred[640]{0:T(1024)(128)(4,1)S(1)} %fusion.278, pred[1280]{0:T(1024)(128)(4,1)S(1)} %fusion.274, f32[1024,2048]{0,1:T(8,128)} %copy-done.1, f32[256,2048]{0,1:T(8,128)S(1)} %copy-done.4), kind=kOutput, calls=%fused_computation.39 | convolution fusion | flops 20137738240 | bytes 22284160 | tf_op jit(solution)/shard_map/dot_general | solution.py:138
  (260 shorter events, 556.5 us)
Async XLA Ops:
  7.2 10.9 copy-start.8
  11.9 64.8 %all-to-all-start = ((f32[2,8,128,512]{3,2,0,1:T(8,128)}), f32[2,8,128,512]{3,2,0,1:T(8,128)}, u32[]{:S(2)}, u32[]{:S(2)}) async-start(f32[2,8,128,512]{3,2,0,1:T(8,128)} %copy.156), calls=%async_computation | async-start | bytes 8388608 | tf_op jit(solution)/shard_map/all_to_all | solution.py:83
  17.8 299.5 %all-gather.3.cloned.1.call-start = ((), (), s32[]{:S(2)}) async-start(), calls=%async_computation.1 | async-start | bytes 16908288 | tf_op jit(solution)/shard_map/all_gather | solution.py:120
  89.3 9.9 copy-start.6
  101.1 234.0 %copy-start.5 = (f32[1280,640]{1,0:T(8,128)}, f32[1280,640]{1,0:T(8,128)S(1)}, u32[]{:S(2)}) copy-start(f32[1280,640]{1,0:T(8,128)S(1)} %bitcast_add_fusion) | copy-start | bytes 9830404
  101.8 741.7 %all-gather.5.cloned.1.call-start = ((), (), s32[]{:S(2)}) async-start(), calls=%async_computation.2 | async-start | bytes 11141120 | tf_op jit(solution)/shard_map/all_gather | solution.py:113
  108.5 1201.3 %all-reduce.4.cloned.1.call-start = ((), (), s32[]{:S(2)}) async-start(), calls=%async_computation.3 | async-start | bytes 10485760 | tf_op jit(solution)/shard_map/psum | solution.py:12
  862.6 35.1 %copy-start.2 = (f32[2,1,128,2048]{3,2,1,0:T(8,128)}, f32[2,1,128,2048]{3,2,1,0:T(8,128)S(1)}, u32[]{:S(2)}) copy-start(f32[2,1,128,2048]{3,2,1,0:T(8,128)S(1)} %constant_dynamic-slice_fusion) | copy-start | bytes 6291460
  875.3 35.9 %slice-start = ((s8[10485760]{0:T(1024)(128)(4,1)}), s8[4194304]{0:T(1024)(128)(4,1)S(1)}, s32[]{:S(2)}) async-start(s8[10485760]{0:T(1024)(128)(4,1)} %bitcast.273), calls=%async_computation.4 | async-start | bytes 8388608
  882.8 28.3 %slice-start.1 = ((s8[10485760]{0:T(1024)(128)(4,1)}), s8[4194304]{0:T(1024)(128)(4,1)S(1)}, s32[]{:S(2)}) async-start(s8[10485760]{0:T(1024)(128)(4,1)} %bitcast.273), calls=%async_computation.5 | async-start | bytes 8388608
  897.7 13.4 slice-start.2
  1007.5 14.4 %copy-start = (f32[1024,2048]{0,1:T(8,128)S(1)}, f32[1024,2048]{0,1:T(8,128)}, u32[]{:S(2)}) copy-start(f32[1024,2048]{0,1:T(8,128)} %fusion.100) | copy-start | bytes 25165828
  1021.8 15.9 %copy-start.7 = (f32[128,128]{1,0:T(8,128)S(1)}, f32[128,128]{1,0:T(8,128)}, u32[]{:S(2)}) copy-start(f32[128,128]{1,0:T(8,128)} %fusion.177) | copy-start | bytes 196612
  1038.3 3.3 copy-start.1
  1082.3 7.2 copy-start.3
  1093.0 216.8 %copy-start.4 = (f32[256,2048]{0,1:T(8,128)S(1)}, f32[256,2048]{0,1:T(8,128)}, u32[]{:S(2)}) copy-start(f32[256,2048]{0,1:T(8,128)} %copy.216) | copy-start | bytes 6291460
Sparse Core Ops, SparseCore 0:
  102.0 215.3 all-gather.2
  320.2 87.1 all-gather.4
  1089.6 220.1 all-reduce.3
where the time goes:
time: 1360 us; the launch traced here: 1350 us
  waiting for transfers between devices  479 us (35%)
  other arithmetic  415 us (31%)
  matrix products  331 us (24%)
  local copies, waits for them, and re-layouts  102 us (8%)
  between operations  15 us (1%)
    psum x1, waiting for transfers between devices, from_root(): return lax.psum(kept, axis)  211 us
    all_gather x1, waiting for transfers between devices, local(): pieces = lax.all_gather(corner, ('row', 'col'), axis=0, tiled=True)  209 us
    another operation x48, other arithmetic, block_cholesky(): diag_factor = jnp.linalg.cholesky(column[:BLK])  200 us
    another operation x32, other arithmetic, block_cholesky(): jax.scipy.linalg.solve_triangular(diag_factor, identity, lower=True)  178 us
    dot_general x15, matrix products, block_solve(): jnp.dot(result[:, :start], factor[start:start + BLK, :start].T, precision...  132 us
    dot_general x15, matrix products, block_cholesky(): jnp.dot(factor[start:, :start], factor[start:start + BLK, :start].T, prec...  77.6 us
    all_to_all x1, waiting for transfers between devices, local(): lax.all_to_all(outgoing, 'row', split_axis=1, concat_axis=1, tiled=True)  58.4 us
    dot_general x16, matrix products, block_solve(): jnp.dot(target, inverses[step].T, precision=lax.Precision.HIGHEST, prefer...  43.4 us
  transfers between devices with their start and end apart: 4, of which 3 were waited for; matrix products, arithmetic and copies ran while one was open for 40% of the time, Pallas kernels for 0%

commit v1 on v0

--- a/solution.py
+++ b/solution.py
@@ -9,7 +9,7 @@
 
 def from_root(value, axis, source):
     kept = jnp.where(lax.axis_index(axis) == source, value, 0).astype(value.dtype)
-    return lax.psum(kept, axis)
+    return jnp.sum(lax.all_gather(kept, axis), axis=0)
 
 
 def block_cholesky(leading):

time: 1360 us -> 1970 us (1.45)
  waiting for transfers between devices: 479 us -> 1060 us
  matrix products: 331 us -> 355 us
    all_gather x0 -> x1, waiting for transfers between devices: none -> 789 us  [from_root(): return jnp.sum(lax.all_gather(kept, axis), axis=0)]
    psum x1 -> x0, waiting for transfers between devices: 211 us -> none  [from_root(): return lax.psum(kept, axis)]
    dot_general x1, matrix products: 31.6 us -> 55 us  [local(): jnp.dot(factor_rows, column_rows.T, precision=lax.Precision.HIGHEST, pref...]
  transfers between devices with their start and end apart: 4 -> 4, of which waited for: 3 -> 3; matrix products, arithmetic and copies ran while one was open for 40% -> 28% of each run, Pallas kernels for 0% -> 0%
where the time goes in v1:
time: 1970 us; the launch traced here: 1960 us
  waiting for transfers between devices  1060 us (54%)
  other arithmetic  420 us (21%)
  matrix products  355 us (18%)
  local copies, waits for them, and re-layouts  106 us (5%)
    all_gather x1, waiting for transfers between devices, from_root(): return jnp.sum(lax.all_gather(kept, axis), axis=0)  789 us
    all_gather x1, waiting for transfers between devices, local(): pieces = lax.all_gather(corner, ('row', 'col'), axis=0, tiled=True)  209 us
    another operation x48, other arithmetic, block_cholesky(): diag_factor = jnp.linalg.cholesky(column[:BLK])  200 us
    another operation x32, other arithmetic, block_cholesky(): jax.scipy.linalg.solve_triangular(diag_factor, identity, lower=True)  178 us
    dot_general x15, matrix products, block_solve(): jnp.dot(result[:, :start], factor[start:start + BLK, :start].T, precision...  132 us
    dot_general x15, matrix products, block_cholesky(): jnp.dot(factor[start:, :start], factor[start:start + BLK, :start].T, prec...  77.6 us
    all_to_all x1, waiting for transfers between devices, local(): lax.all_to_all(outgoing, 'row', split_axis=1, concat_axis=1, tiled=True)  58.4 us
    dot_general x1, matrix products, local(): jnp.dot(factor_rows, column_rows.T, precision=lax.Precision.HIGHEST, pref...  55 us
  transfers between devices with their start and end apart: 4, of which 3 were waited for; matrix products, arithmetic and copies ran while one was open for 28% of the time, Pallas kernels for 0%

profile of v1, /device:TPU:1, one launch (start us, length us, event | category | flops | bytes accessed | tf_op | source)
XLA Modules:
  0.0 1957.4 jit_solution(17670833727957370574)
XLA Ops:
  18.3 58.4 %all-to-all-done = f32[2,8,128,512]{3,2,0,1:T(8,128)} async-done(((f32[2,8,128,512]{3,2,0,1:T(8,128)}), f32[2,8,128,512]{3,2,0,1:T(8,128)}, u32[]{:S(2)}, u32[]{:S(2)}) %all-to-all-start) | async-done | bytes 4194336 | tf_op jit(solution)/shard_map/all_to_all | solution.py:83
  108.5 208.7 %all-gather.4.cloned.1.call-done = f32[32768,128]{1,0:T(8,128)} async-done(((f32[256,128]{1,0:T(8,128)}), f32[32768,128]{1,0:T(8,128)}) %all-gather.4.cloned.1.call-update) | async-done | bytes 16777232 | tf_op jit(solution)/shard_map/all_gather | solution.py:120
  317.3 17.8 copy.165
  335.0 18.0 reshape.1466
  354.8 11.7 cholesky.254
  392.1 11.9 cholesky.265
  422.5 11.7 cholesky.276
  453.9 11.7 cholesky.287
  486.1 11.7 cholesky.298
  518.2 11.7 cholesky.309
  550.9 11.7 cholesky.320
  583.4 12.1 cholesky.331
  616.5 11.9 cholesky.342
  648.6 11.9 cholesky.353
  772.7 11.9 cholesky.397
  975.0 12.6 fusion.71
  990.6 13.4 fusion.74
  1007.1 14.3 fusion.124
  1022.9 14.6 fusion.77
  1047.8 13.3 reshape.1470
  1069.8 11.8 copy.201
  1089.2 788.9 %all-gather.8.cloned.1.call-done = f32[8,640,2048]{2,1,0:T(8,128)} async-done(((f32[1,640,2048]{2,1,0:T(8,128)}), f32[8,640,2048]{2,1,0:T(8,128)}) %all-gather.8.cloned.1.call-update) | async-done | bytes 41943056 | tf_op jit(solution)/shard_map/all_gather | solution.py:12
  1878.2 17.3 reduce_sum.29
  1895.4 55.0 %fusion.32 = f32[1280,640]{1,0:T(8,128)} fusion(f32[1280,640]{1,0:T(8,128)} %copy-done.5, f32[640,2048]{1,0:T(8,128)} %reduce_sum.29, pred[640]{0:T(1024)(128)(4,1)S(1)} %fusion.277, pred[1280]{0:T(1024)(128)(4,1)S(1)} %fusion.273, f32[1024,2048]{0,1:T(8,128)} %copy-done.1, f32[256,2048]{0,1:T(8,128)S(1)} %copy-done.4), kind=kOutput, calls=%fused_computation.37 | convolution fusion | flops 20137738240 | bytes 22284160 | tf_op jit(solution)/shard_map/dot_general | solution.py:138
  (261 shorter events, 568.1 us)
Async XLA Ops:
  7.2 10.9 copy-start.8
  11.9 64.8 %all-to-all-start = ((f32[2,8,128,512]{3,2,0,1:T(8,128)}), f32[2,8,128,512]{3,2,0,1:T(8,128)}, u32[]{:S(2)}, u32[]{:S(2)}) async-start(f32[2,8,128,512]{3,2,0,1:T(8,128)} %copy.160), calls=%async_computation | async-start | bytes 8388608 | tf_op jit(solution)/shard_map/all_to_all | solution.py:83
  17.8 299.5 %all-gather.4.cloned.1.call-start = ((), (), s32[]{:S(2)}) async-start(), calls=%async_computation.1 | async-start | bytes 16908288 | tf_op jit(solution)/shard_map/all_gather | solution.py:120
  89.3 9.9 copy-start.6
  101.0 234.0 %copy-start.5 = (f32[1280,640]{1,0:T(8,128)}, f32[1280,640]{1,0:T(8,128)S(1)}, u32[]{:S(2)}) copy-start(f32[1280,640]{1,0:T(8,128)S(1)} %bitcast_add_fusion) | copy-start | bytes 9830404
  101.8 741.5 %all-gather.6.cloned.1.call-start = ((), (), s32[]{:S(2)}) async-start(), calls=%async_computation.2 | async-start | bytes 11141120 | tf_op jit(solution)/shard_map/all_gather | solution.py:113
  108.5 1769.7 %all-gather.8.cloned.1.call-start = ((), (), s32[]{:S(2)}) async-start(), calls=%async_computation.3 | async-start | bytes 47185920 | tf_op jit(solution)/shard_map/all_gather | solution.py:12
  862.3 35.0 %copy-start.2 = (f32[2,1,128,2048]{3,2,1,0:T(8,128)}, f32[2,1,128,2048]{3,2,1,0:T(8,128)S(1)}, u32[]{:S(2)}) copy-start(f32[2,1,128,2048]{3,2,1,0:T(8,128)S(1)} %constant_dynamic-slice_fusion) | copy-start | bytes 6291460
  874.9 35.9 %slice-start = ((s8[10485760]{0:T(1024)(128)(4,1)}), s8[4194304]{0:T(1024)(128)(4,1)S(1)}, s32[]{:S(2)}) async-start(s8[10485760]{0:T(1024)(128)(4,1)} %bitcast.267), calls=%async_computation.4 | async-start | bytes 8388608
  882.4 28.4 %slice-start.1 = ((s8[10485760]{0:T(1024)(128)(4,1)}), s8[4194304]{0:T(1024)(128)(4,1)S(1)}, s32[]{:S(2)}) async-start(s8[10485760]{0:T(1024)(128)(4,1)} %bitcast.267), calls=%async_computation.5 | async-start | bytes 8388608
  897.3 13.5 slice-start.2
  1007.1 14.4 copy-start
  1021.5 16.0 copy-start.7
  1038.1 3.2 copy-start.1
  1069.8 11.8 copy-start.3
  1089.2 806.2 %copy-start.4 = (f32[256,2048]{0,1:T(8,128)S(1)}, f32[256,2048]{0,1:T(8,128)}, u32[]{:S(2)}) copy-start(f32[256,2048]{0,1:T(8,128)} %copy.222) | copy-start | bytes 6291460
Sparse Core Ops, SparseCore 0:
  101.9 215.3 all-gather.3
  320.1 87.2 all-gather.5
  1081.7 796.4 all-gather.7
